TPU v7x, 32 devices: a whole 2x2x4 slice. The times are simulated.
32 devices in a mesh: dp: 4 (over y, core), own: 8 (over z, x).
Axes of the slice: x: 2, y: 2, z: 4, core: 2. Of those that a mesh axis runs over, the one named last changes fastest.
Arguments:
- grads: bfloat16 [4, 16, 768, 768], P('dp', 'own'), may hold values from -0.059814453 to 0.059814453
- owner: int32 [16], replicated, may hold values from 0 to 7, as said below
- weights: float32 [32, 768, 768], P('own', 'dp'), may hold values from -6 to 6
- stat_left: float32 [32, 768, 768], P('own', 'dp'), may hold values from -3 to 3
- stat_right: float32 [32, 768, 768], P('own', 'dp'), may hold values from -3 to 3
- adam_second: float32 [32, 768, 768], P('own', 'dp'), may hold values from 0.0002 to 1
- root_left: bfloat16 [32, 768, 768], P('own', 'dp'), may hold values from -0.21875 to 0.21875
- root_right: bfloat16 [32, 768, 768], P('own', 'dp'), may hold values from -0.21875 to 0.21875
Outputs:
- new_weights: bfloat16 [32, 768, 768], P('own')
- new_left: float32 [32, 768, 768], P('own', 'dp')
- new_right: float32 [32, 768, 768], P('own', 'dp')
- new_second: float32 [32, 768, 768], P('own', 'dp')
Inputs may be any that keep to these rules, and one draw needn't show every extreme that they name: The 2 blocks 2 * j to 2 * j + 1 have different owners, for every j; one owner holds exactly 4 blocks and none holds more.
All inputs are finite; a program needn't handle non-finite values.
Results may differ from a plain program's by a relative error of at most 0.0095.
Values may be sent and summed in bfloat16 or wider, within the bound.
A program may use at most 64 MiB of HBM per device.

v0:
```python
import jax
import jax.numpy as jnp
from jax import lax
from jax.sharding import PartitionSpec as P


def slot_index(owner, capacity):
    count = owner.shape[0]
    same = owner[:, None] == owner[None, :]
    earlier = (
        jnp.arange(count, dtype=jnp.int32)[None, :] < jnp.arange(count, dtype=jnp.int32)[:, None]
    )
    rank = jnp.sum((same & earlier).astype(jnp.int32), axis=1)
    return owner * capacity + rank


def on_device(grads, owner, weights, stat_left, stat_right, adam_second, root_left, root_right):
    per_index = grads.shape[1]
    width = grads.shape[3]
    capacity = 2 * per_index
    replicas = lax.axis_size("dp")
    me = lax.axis_index("own")
    rep = lax.axis_index("dp")
    col_count = width // replicas
    summed = lax.psum_scatter(
        grads[0].astype(jnp.float32).astype(jnp.bfloat16), "dp", scatter_dimension=1, tiled=True
    )
    row_count = summed.shape[1]
    slot = slot_index(owner, capacity)
    targets = me * capacity + jnp.arange(capacity, dtype=jnp.int32)
    every = lax.all_gather(summed, "own", axis=0, tiled=True)
    pick = (slot[None, :] == targets[:, None]).astype(jnp.bfloat16)
    mine = jnp.dot(
        pick, every.reshape(every.shape[0], row_count * width), preferred_element_type=jnp.float32
    )
    mine = mine.astype(jnp.bfloat16).reshape(capacity, row_count, width)
    full = lax.all_gather(mine, "dp", axis=1, tiled=True)
    new_left = 0.5 * stat_left + 0.5 * jnp.einsum(
        "srd,sbd->srb", mine, full, preferred_element_type=jnp.float32
    )
    columns = lax.dynamic_slice_in_dim(full, rep * col_count, col_count, 2)
    new_right = 0.5 * stat_right + 0.5 * jnp.einsum(
        "sbc,sbd->scd", columns, full, preferred_element_type=jnp.float32
    )
    grad32 = mine.astype(jnp.float32)
    new_second = 0.9 * adam_second + 0.1 * grad32 * grad32
    adam_dir = grad32 / (jnp.sqrt(new_second) + 1e-08)
    half = jnp.einsum("srb,sbd->srd", root_left, full, preferred_element_type=jnp.float32).astype(
        jnp.bfloat16
    )
    precond = jnp.einsum(
        "src,scd->srd",
        half,
        lax.all_gather(root_right, "dp", axis=1, tiled=True),
        preferred_element_type=jnp.float32,
    )
    adam_sq = jnp.sum(adam_dir * adam_dir, axis=(1, 2))
    prec_sq = jnp.sum(precond * precond, axis=(1, 2))
    adam_total, prec_total = lax.psum((adam_sq, prec_sq), "dp")
    graft = jnp.sqrt(adam_total) / (jnp.sqrt(prec_total) + 1e-06)
    fresh_rows = (weights - graft[:, None, None] * precond).astype(jnp.bfloat16)
    new_weights = lax.all_gather(fresh_rows, "dp", axis=1, tiled=True)
    return (new_weights, new_left, new_right, new_second)


def solution(mesh):
    placed = (
        P("dp", "own", None, None),
        P(),
        P("own", "dp", None),
        P("own", "dp", None),
        P("own", "dp", None),
        P("own", "dp", None),
        P("own", "dp", None),
        P("own", "dp", None),
    )
    return jax.shard_map(
        on_device,
        mesh=mesh,
        in_specs=placed,
        out_specs=(
            P("own", None, None),
            P("own", "dp", None),
            P("own", "dp", None),
            P("own", "dp", None),
        ),
        check_vma=False,
    )
```

profile of v0, /device:TPU:0, one launch (start us, length us, event | category | flops | bytes accessed | tf_op | source)
XLA Modules:
  0.0 272.5 jit_solution(467459611069070549)
XLA Ops:
  7.2 0.0 copy-start
  7.2 0.0 copy-start.2
  7.2 0.0 reduce-scatter.2.cloned.1.call-start
  7.2 0.7 reduce-scatter.2.cloned.1.call-update
  7.9 0.0 all-gather.5.cloned.1.call-start
  8.0 38.4 %reduce-scatter.2.cloned.1.call-done = bf16[2,192,768]{2,1,0:T(8,128)(2,1)} async-done(((bf16[2,768,768]{2,1,0:T(8,128)(2,1)}), bf16[2,192,768]{2,1,0:T(8,128)(2,1)}) %reduce-scatter.2.cloned.1.call-update) | async-done | bytes 589840 | tf_op jit(solution)/shard_map/reduce_scatter | solution.py:25
  46.3 0.0 all-gather.5.cloned.1.call-update
  46.4 0.0 all-gather.9.cloned.1.call-start
  46.4 0.7 all-gather.9.cloned.1.call-update
  47.1 0.0 all-gather.7.cloned.1.call-start
  47.2 0.2 convert_reduce_fusion
  47.4 81.3 %all-gather.5.cloned.1.call-done = bf16[16,192,768]{2,1,0:T(8,128)(2,1)} async-done(((bf16[2,192,768]{2,1,0:T(8,128)(2,1)}), bf16[16,192,768]{2,1,0:T(8,128)(2,1)}) %all-gather.5.cloned.1.call-update) | async-done | bytes 4718608 | tf_op jit(solution)/shard_map/all_gather | solution.py:31
  128.7 5.0 %copy.16 = bf16[2,8,192,768]{3,1,2,0:T(8,128)(2,1)S(1)} copy(bf16[2,8,192,768]{3,2,1,0:T(8,128)(2,1)} %bitcast.25) | data formatting | bytes 9437184
  133.6 0.9 convolution_convert_fusion
  134.6 1.1 copy.25
  135.7 0.0 all-gather.7.cloned.1.call-update
  135.7 0.0 all-gather.11.cloned.1.call-start
  135.8 4.6 %fusion.2 = (f32[4]{0:T(128)S(1)}, f32[4,192,768]{2,1,0:T(8,128)}) fusion(bf16[1,4,192,768]{3,1,2,0:T(4,128)(2,1)S(1)} %bitcast.23, f32[4,192,768]{2,1,0:T(8,128)} %param.13), kind=kLoop, calls=%fused_computation.9 | loop fusion | flops 5308412 | bytes 5898256 | tf_op jit(solution)/shard_map/reduce_sum | solution.py:57
  140.3 25.6 %all-gather.9.cloned.1.call-done = bf16[4,768,768]{2,1,0:T(8,128)(2,1)} async-done(((bf16[4,192,768]{2,1,0:T(8,128)(2,1)}), bf16[4,768,768]{2,1,0:T(8,128)(2,1)}) %all-gather.9.cloned.1.call-update) | async-done | bytes 4718608 | tf_op jit(solution)/shard_map/all_gather | solution.py:54
  166.0 39.6 %all-gather.7.cloned.1.call-done = bf16[4,768,768]{2,1,0:T(8,128)(2,1)} async-done(((bf16[4,192,768]{2,1,0:T(8,128)(2,1)}), bf16[4,768,768]{2,1,0:T(8,128)(2,1)}) %all-gather.7.cloned.1.call-update) | async-done | bytes 4718608 | tf_op jit(solution)/shard_map/all_gather | solution.py:37
  205.5 7.2 %multiply_reduce_fusion = (f32[4]{0:T(128)S(1)}, f32[4,192,768]{2,1,0:T(8,128)}) fusion(bf16[4,768,768]{2,1,0:T(8,128)(2,1)} %all-gather.9.cloned.1.call-done, bf16[4,192,768]{2,1,0:T(8,128)(2,1)S(1)} %copy-done, bf16[4,768,768]{2,1,0:T(8,128)(2,1)} %all-gather.7.cloned.1.call-done), kind=kOutput, calls=%fused_computation.8 | convolution fusion | flops 1813708800 | bytes 12976144 | tf_op jit(solution)/shard_map/src,scd->srd/dot_general | solution.py:51
  212.7 5.9 %all-reduce = (f32[4]{0:T(128)S(1)}, f32[4]{0:T(128)S(1)}) all-reduce(f32[4]{0:T(128)S(1)} %get-tuple-element.8, f32[4]{0:T(128)S(1)} %get-tuple-element.6), channel_id=1, replica_groups=mesh['dp'=4,'own'=8] {'dp'}, use_global_device_ids=true, to_apply=%region_5.0 | all-reduce | flops 8 | bytes 64 | tf_op jit(solution)/shard_map/psum | solution.py:59
  218.6 3.8 %subtract_convert_fusion = bf16[4,192,768]{2,1,0:T(8,128)(2,1)} fusion(f32[4,192,768]{2,1,0:T(8,128)} %param.10, f32[4,192,768]{2,1,0:T(8,128)} %get-tuple-element.9, f32[4]{0:T(128)S(1)} %add_divide_fusion), kind=kLoop, calls=%fused_computation.7 | loop fusion | flops 1769472 | bytes 5898256 | tf_op jit(solution)/shard_map/convert_element_type | solution.py:61
  222.4 0.0 all-gather.11.cloned.1.call-update
  222.5 0.0 slice-start.1
  222.5 0.0 copy-start.1
  222.5 7.0 %add_multiply_fusion = f32[4,192,768]{2,1,0:T(8,128)} fusion(f32[4,192,768]{2,1,0:T(8,128)} %param.12, bf16[4,768,768]{2,1,0:T(8,128)(2,1)} %all-gather.7.cloned.1.call-done, s32[]{:T(128)S(6)} %select_n.3), kind=kOutput, calls=%fused_computation.5 | convolution fusion | flops 907149312 | bytes 11010052 | tf_op jit(solution)/shard_map/sbc,sbd->scd/dot_general | solution.py:42
  229.5 0.0 slice-done
  229.5 0.0 copy-done.1
  229.5 3.1 %add_multiply_fusion.1 = f32[4,192,768]{2,1,0:T(8,128)} fusion(f32[4,192,768]{2,1,0:T(8,128)S(1)} %copy-done.1, bf16[4,768,768]{2,1,0:T(8,128)(2,1)S(1)} %bitcast.20, bf16[1,4,192,768]{3,1,2,0:T(4,128)(2,1)S(1)} %bitcast.24), kind=kOutput, calls=%fused_computation.6 | convolution fusion | flops 907149312 | bytes 10616832 | tf_op jit(solution)/shard_map/srd,sbd->srb/dot_general | solution.py:38
  232.6 28.5 %all-gather.11.cloned.1.call-done = bf16[4,768,768]{2,1,0:T(8,128)(2,1)} async-done(((bf16[4,192,768]{2,1,0:T(8,128)(2,1)}), bf16[4,768,768]{2,1,0:T(8,128)(2,1)}) %all-gather.11.cloned.1.call-update) | async-done | bytes 4718608 | tf_op jit(solution)/shard_map/all_gather | solution.py:62
  261.2 4.8 %copy.27 = bf16[4,768,768]{2,1,0:T(8,128)(2,1)} copy(bf16[4,768,768]{2,1,0:T(8,128)(2,1)} %all-gather.11.cloned.1.call-done) | data formatting | bytes 9437184
  (8 shorter events, 0.0 us)
Async XLA Ops:
  7.2 198.4 %copy-start = (bf16[4,192,768]{2,1,0:T(8,128)(2,1)S(1)}, bf16[4,192,768]{2,1,0:T(8,128)(2,1)}, u32[]{:S(2)}) copy-start(bf16[4,192,768]{2,1,0:T(8,128)(2,1)} %param.14) | copy-start | bytes 3538948
  7.2 40.0 %copy-start.2 = (s32[16]{0:T(128)S(1)}, s32[16]{0:T(128)}, u32[]{:S(2)}) copy-start(s32[16]{0:T(128)} %param.9) | copy-start | bytes 196
  7.2 39.1 %reduce-scatter.2.cloned.1.call-start = ((), (), s32[]{:S(2)}) async-start(), calls=%async_computation.1 | async-start | bytes 2949120 | tf_op jit(solution)/shard_map/reduce_scatter | solution.py:25
  7.9 120.8 %all-gather.5.cloned.1.call-start = ((), (), s32[]{:S(2)}) async-start(), calls=%async_computation.2 | async-start | bytes 5308416 | tf_op jit(solution)/shard_map/all_gather | solution.py:31
  46.4 119.6 %all-gather.9.cloned.1.call-start = ((), (), s32[]{:S(2)}) async-start(), calls=%async_computation.4 | async-start | bytes 5898240 | tf_op jit(solution)/shard_map/all_gather | solution.py:54
  47.1 158.4 %all-gather.7.cloned.1.call-start = ((), (), s32[]{:S(2)}) async-start(), calls=%async_computation.3 | async-start | bytes 5898240 | tf_op jit(solution)/shard_map/all_gather | solution.py:37
  135.7 125.4 %all-gather.11.cloned.1.call-start = ((), (), s32[]{:S(2)}) async-start(), calls=%async_computation.5 | async-start | bytes 5898240 | tf_op jit(solution)/shard_map/all_gather | solution.py:62
  222.4 7.0 %slice-start = ((s8[4718592]{0:T(1024)(128)(4,1)}), s8[524288]{0:T(1024)(128)(4,1)S(1)}, s32[]{:S(2)}) async-start(s8[4718592]{0:T(1024)(128)(4,1)} %bitcast.19), calls=%async_computation.6 | async-start | bytes 1048576
  222.5 7.0 %slice-start.1 = ((s8[4718592]{0:T(1024)(128)(4,1)}), s8[4194304]{0:T(1024)(128)(4,1)S(1)}, s32[]{:S(2)}) async-start(s8[4718592]{0:T(1024)(128)(4,1)} %bitcast.19), calls=%async_computation.7 | async-start | bytes 8388608
  222.5 7.0 %copy-start.1 = (f32[4,192,768]{2,1,0:T(8,128)S(1)}, f32[4,192,768]{2,1,0:T(8,128)}, u32[]{:S(2)}) copy-start(f32[4,192,768]{2,1,0:T(8,128)} %param.11) | copy-start | bytes 7077892
Sparse Core Ops, SparseCore 0:
  10.6 35.7 reduce-scatter.1
  48.8 79.8 all-gather.4
  130.3 35.5 all-gather.8
  168.0 37.4 all-gather.6
  222.6 38.5 all-gather.10
where the time goes:
time: 273 us
  waiting for transfers between devices  215 us (79%)
  matrix products  18.2 us (7%)
  between operations  13.9 us (5%)
  local copies, waits for them, and re-layouts  10.9 us (4%)
  other arithmetic  8.62 us (3%)
  blocking collectives  5.87 us (2%)
    all_gather x1, waiting for transfers between devices, on_device(): every = lax.all_gather(summed, 'own', axis=0, tiled=True)  81.3 us
    all_gather x1, waiting for transfers between devices, on_device(): full = lax.all_gather(mine, 'dp', axis=1, tiled=True)  39.6 us
    reduce_scatter x1, waiting for transfers between devices, on_device(): lax.psum_scatter(grads[0].astype(jnp.float32).astype(jnp.bfloat16), 'dp',...  38.4 us
    all_gather x1, waiting for transfers between devices, on_device(): new_weights = lax.all_gather(fresh_rows, 'dp', axis=1, tiled=True)  28.5 us
    all_gather x1, waiting for transfers between devices, on_device(): lax.all_gather(root_right, 'dp', axis=1, tiled=True)  25.6 us
    unnamed x13, local copies, waits for them, and re-layouts  10.9 us
    dot_general x1, matrix products, on_device(): jnp.einsum('src,scd->srd', half, lax.all_gather(root_right, 'dp', axis=1,...  7.19 us
    dot_general x1, matrix products, on_device(): jnp.einsum('sbc,sbd->scd', columns, full, preferred_element_type=jnp.floa...  6.97 us
  transfers between devices with their start and end apart: 5, of which 5 were waited for; matrix products, arithmetic and copies ran while one was open for 8% of the time, Pallas kernels for 0%

commit v1 on v0

v1 whole, which is shorter than its diff:
```python
import functools

import jax
import jax.numpy as jnp
from jax import lax
from jax.experimental import pallas as pl
from jax.experimental.pallas import tpu as pltpu
from jax.sharding import PartitionSpec as P

MESH = pl.DeviceIdType.MESH
PAIR = 2


def dot(a, b):
    return lax.dot_general(a, b, (((1,), (0,)), ((), ())), preferred_element_type=jnp.float32)


def dot_nt(a, b):
    return lax.dot_general(a, b, (((1,), (1,)), ((), ())), preferred_element_type=jnp.float32)


def kernel(
    replicas,
    owners,
    owner_ref,
    grads,
    weights,
    stat_left,
    stat_right,
    adam_second,
    root_left,
    root_right,
    out_weights,
    out_left,
    out_right,
    out_second,
    own_rows,
    core_in,
    part_out,
    part_in,
    blocks,
    cross_out,
    cross_in,
    full,
    roots,
    left_v,
    right_v,
    second_v,
    weights_v,
    root_v,
    precond,
    fresh,
    norm_out,
    norm_in,
    load_sem,
    own_sem,
    store_sem,
    core_s,
    core_r,
    part_s,
    part_r,
    up_s,
    down_s,
    block_r,
    cross_s,
    cross_r,
    grad_sems,
    root_sems,
    weight_sems,
    norm_s,
    norm_r,
):
    outer = replicas // PAIR
    layers = owners // PAIR
    per_index = grads.shape[1]
    count = per_index * owners
    capacity = weights.shape[0]
    rows = weights.shape[1]
    me = lax.axis_index("dp")
    mine = lax.axis_index("own")
    y, c = lax.div(me, PAIR), lax.rem(me, PAIR)
    o, i = lax.div(mine, PAIR), lax.rem(mine, PAIR)
    f32, bf16 = jnp.float32, jnp.bfloat16

    def replica(yy, cc):
        return {"dp": yy * PAIR + cc, "own": mine}

    def group(oo, ii):
        return {"dp": me, "own": oo * PAIR + ii}

    def span(yy, cc):
        return pl.ds(pl.multiple_of((yy * PAIR + cc) * rows, rows), rows)

    def shifted(k):
        return lax.rem(y + k, outer)

    def back(k):
        return lax.rem(y + outer - k, outer)

    def remote(src, dst, send, recv, device):
        return pltpu.make_async_remote_copy(
            src_ref=src,
            dst_ref=dst,
            send_sem=send,
            recv_sem=recv,
            device_id=device,
            device_id_type=MESH,
        )

    core_peer = replica(y, 1 - c)
    cross_peer = group(o, 1 - i)
    above, below = o + 1 < layers, o >= 1

    own_copies = {}
    for b in range(per_index):
        for k in range(outer):
            copy = pltpu.make_async_copy(
                grads.at[0, b, span(shifted(k), c)], own_rows.at[b, k], own_sem.at[b, k]
            )
            copy.start()
            own_copies[b, k] = copy

    barrier = pltpu.get_barrier_semaphore()
    for k in range(1, replicas):
        pl.semaphore_signal(
            barrier,
            inc=1,
            device_id={"dp": lax.rem(me + k, replicas), "own": mine},
            device_id_type=MESH,
        )
    pl.semaphore_signal(barrier, inc=1, device_id=cross_peer, device_id_type=MESH)

    @pl.when(above)
    def _():
        pl.semaphore_signal(barrier, inc=1, device_id=group(o + 1, i), device_id_type=MESH)

    @pl.when(below)
    def _():
        pl.semaphore_signal(barrier, inc=1, device_id=group(o - 1, i), device_id_type=MESH)

    lines = above.astype(jnp.int32) + below.astype(jnp.int32)
    pl.semaphore_wait(barrier, replicas + lines)

    order = list(range(1, outer)) + [0]
    core_copies = {}
    for b in range(per_index):
        for k in order:
            copy = remote(
                grads.at[0, b, span(shifted(k), 1 - c)],
                core_in.at[b, k],
                core_s.at[b, k],
                core_r.at[b, k],
                core_peer,
            )
            copy.start()
            core_copies[b, k] = copy

    loads = [
        pltpu.make_async_copy(root_right, roots.at[:, span(y, c)], load_sem.at[0]),
        pltpu.make_async_copy(adam_second, second_v, load_sem.at[1]),
        pltpu.make_async_copy(root_left, root_v, load_sem.at[2]),
        pltpu.make_async_copy(weights, weights_v, load_sem.at[3]),
        pltpu.make_async_copy(stat_left, left_v, load_sem.at[4]),
        pltpu.make_async_copy(stat_right, right_v, load_sem.at[5]),
    ]
    for copy in loads:
        copy.start()

    part_copies = []
    for b in range(per_index):
        for k in range(1, outer):
            own_copies[b, k].wait()
            core_copies[b, k].wait_recv()
            part_out[b, k - 1] = (
                own_rows[b, k].astype(f32) + core_in[b, k].astype(f32)
            ).astype(bf16)
            copy = remote(
                part_out.at[b, k - 1],
                part_in.at[b, k - 1],
                part_s.at[b, k - 1],
                part_r.at[b, k - 1],
                replica(shifted(k), c),
            )
            copy.start()
            part_copies.append(copy)

    def far_copy(src, ref, s, k, sems):
        return remote(
            src, ref.at[s, span(y, c)], sems.at[0, s, k], sems.at[1, s, k], replica(shifted(k), c)
        )

    def near_copy(src, ref, s, k, sems):
        return remote(
            src, ref.at[s, span(back(k), c)], sems.at[2, s, k], sems.at[3, s, k], core_peer
        )

    def gather_start(src, ref, s, sems):
        for k in range(1, outer):
            far_copy(src, ref, s, k, sems).start()
        near_copy(src, ref, s, 0, sems).start()

    def gather_forward(ref, s, sems):
        for k in range(1, outer):
            landed = ref.at[s, span(back(k), c)]
            remote(landed, landed, sems.at[0, s, k], sems.at[1, s, k], core_peer).wait_recv()
            near_copy(landed, ref, s, k, sems).start()

    def gather_arrived(ref, s, sems):
        for k in range(outer):
            landed = ref.at[s, span(back(k), 1 - c)]
            remote(landed, landed, sems.at[2, s, k], sems.at[3, s, k], core_peer).wait_recv()

    def gather_sent(src, ref, s, sems):
        for k in range(1, outer):
            far_copy(src, ref, s, k, sems).wait_send()
        for k in range(outer):
            near_copy(src, ref, s, k, sems).wait_send()

    def slots(body):
        def step(s, carry):
            body(s)
            return carry

        lax.fori_loop(0, capacity, step, 0)

    loads[0].wait()
    slots(lambda s: gather_start(roots.at[s, span(y, c)], roots, s, root_sems))

    def send_up(src, k, b):
        return remote(
            blocks.at[src, b],
            blocks.at[src, b],
            up_s.at[k, b],
            block_r.at[src, b],
            group(o + 1, i),
        )

    def send_down(src, k, b):
        return remote(
            blocks.at[src, b],
            blocks.at[src, b],
            down_s.at[k, b],
            block_r.at[src, b],
            group(o - 1, i),
        )

    def wait_block(src, b):
        remote(
            blocks.at[src, b], blocks.at[src, b], up_s.at[0, b], block_r.at[src, b], cross_peer
        ).wait_recv()

    def cross_copy(src):
        return remote(
            cross_out.at[src], cross_in.at[src], cross_s.at[src], cross_r.at[src], cross_peer
        )

    def cross(src):
        first = (src * PAIR + i) * per_index
        other = o * PAIR + 1 - i
        sent = blocks[src, 0]
        for b in range(1, per_index):
            sent = jnp.where(owner_ref[first + b] == other, blocks[src, b], sent)
        cross_out[src] = sent
        cross_copy(src).start()

    for b in range(per_index):
        own_copies[b, 0].wait()
        core_copies[b, 0].wait_recv()
        total = own_rows[b, 0].astype(f32) + core_in[b, 0].astype(f32)
        for k in range(1, outer):
            remote(
                part_out.at[b, k - 1],
                part_in.at[b, k - 1],
                part_s.at[b, k - 1],
                part_r.at[b, k - 1],
                core_peer,
            ).wait_recv()
            total = total + part_in[b, k - 1].astype(f32)
        blocks[o, b] = total.astype(bf16)

        @pl.when(above)
        def _():
            send_up(o, 0, b).start()

        @pl.when(below)
        def _():
            send_down(o, 0, b).start()

    cross(o)
    for d in range(1, layers):
        for b in range(per_index):

            @pl.when(o >= d)
            def _():
                wait_block(o - d, b)

                @pl.when(above)
                def _():
                    send_up(o - d, d, b).start()

            @pl.when(o + d < layers)
            def _():
                wait_block(o + d, b)

                @pl.when(below)
                def _():
                    send_down(o + d, d, b).start()

        @pl.when(o >= d)
        def _():
            cross(o - d)

        @pl.when(o + d < layers)
        def _():
            cross(o + d)

    slots(lambda s: gather_forward(roots, s, root_sems))
    for src in range(layers):
        cross_copy(src).wait_recv()

    def choose(s):
        found = jnp.int32(0)
        seen = jnp.int32(0)
        valid = jnp.int32(0)
        for b in range(count):
            hit = (owner_ref[b] == mine).astype(jnp.int32)
            take = hit * (seen == s).astype(jnp.int32)
            found = found + take * b
            valid = valid + take
            seen = seen + hit
        source = lax.div(found, per_index)
        layer, side = lax.div(source, PAIR), lax.rem(source, PAIR)
        straight = blocks[layer, lax.rem(found, per_index)]
        crossed = cross_in[layer]
        picked = jnp.where(side == i, straight, crossed)
        full[s, span(y, c)] = jnp.where(valid == 1, picked, jnp.zeros_like(picked))
        gather_start(full.at[s, span(y, c)], full, s, grad_sems)

    slots(choose)
    for copy in loads[1:]:
        copy.wait()

    def store(ref, out, which, s):
        return pltpu.make_async_copy(ref.at[s], out.at[s], store_sem.at[which, s])

    row_of = lax.broadcasted_iota(jnp.int32, (8, 128), 0)

    def norm_copy(s, k):
        return remote(
            norm_out.at[s],
            norm_in.at[k - 1, s],
            norm_s.at[s, k - 1],
            norm_r.at[s, k - 1],
            {"dp": lax.rem(me + k, replicas), "own": mine},
        )

    def own_output(s):
        return pltpu.make_async_copy(
            fresh.at[s], out_weights.at[s, span(y, c)], store_sem.at[3, s]
        )

    def update(s):
        norms = norm_out[s]
        for k in range(1, replicas):
            norm_copy(s, k).wait_recv()
            norms = norms + norm_in[k - 1, s]
        graft = jnp.sqrt(norms[0:1, 0:1]) / (jnp.sqrt(norms[4:5, 0:1]) + 1e-06)
        fresh[s] = (weights_v[s] - graft * precond[s]).astype(bf16)
        gather_start(fresh.at[s], out_weights, s, weight_sems)
        own_output(s).start()

    def precondition(s):
        grad32 = full[s, span(y, c)].astype(f32)
        second = 0.9 * second_v[s] + 0.1 * grad32 * grad32
        second_v[s] = second
        store(second_v, out_second, 0, s).start()
        direction = grad32 / (jnp.sqrt(second) + 1e-08)
        adam_sq = jnp.sum(direction * direction)
        gather_forward(full, s, grad_sems)
        gather_arrived(full, s, grad_sems)
        gather_arrived(roots, s, root_sems)
        half = dot(root_v[s], full[s]).astype(bf16)
        result = dot(half, roots[s])
        precond[s] = result
        norm_out[s] = jnp.where(row_of < 4, adam_sq, jnp.sum(result * result))
        for k in range(1, replicas):
            norm_copy(s, k).start()

        @pl.when(s >= 1)
        def _():
            update(s - 1)

    slots(precondition)
    update(capacity - 1)

    width = full.shape[2]
    cols = width // replicas
    shape = (cols, width)
    pick = (
        lax.broadcasted_iota(jnp.int32, shape, 1)
        == lax.broadcasted_iota(jnp.int32, shape, 0) + me * cols
    ).astype(f32).astype(bf16)

    def statistics(s):
        left_v[s] = 0.5 * left_v[s] + 0.5 * dot_nt(full[s, span(y, c)], full[s])
        store(left_v, out_left, 1, s).start()
        columns = dot_nt(pick, full[s]).astype(bf16)
        right_v[s] = 0.5 * right_v[s] + 0.5 * dot(columns, full[s])
        store(right_v, out_right, 2, s).start()
        gather_forward(out_weights, s, weight_sems)

    slots(statistics)

    for copy in list(core_copies.values()) + part_copies:
        copy.wait_send()
    for k in range(layers - 1):
        for b in range(per_index):

            @pl.when(above & (o >= k))
            def _():
                send_up(o - k, k, b).wait_send()

            @pl.when(below & (o + k < layers))
            def _():
                send_down(o + k, k, b).wait_send()

    for src in range(layers):
        cross_copy(src).wait_send()

    def finish(s):
        gather_sent(roots.at[s, span(y, c)], roots, s, root_sems)
        gather_sent(full.at[s, span(y, c)], full, s, grad_sems)
        for k in range(1, replicas):
            norm_copy(s, k).wait_send()
        store(second_v, out_second, 0, s).wait()
        store(left_v, out_left, 1, s).wait()
        store(right_v, out_right, 2, s).wait()
        own_output(s).wait()
        gather_arrived(out_weights, s, weight_sems)
        gather_sent(fresh.at[s], out_weights, s, weight_sems)

    slots(finish)


def on_device(
    replicas,
    owners,
    grads,
    owner,
    weights,
    stat_left,
    stat_right,
    adam_second,
    root_left,
    root_right,
):
    capacity, rows, width = weights.shape
    per_index, height = grads.shape[1], grads.shape[2]
    outer, layers = replicas // PAIR, owners // PAIR
    bf16, f32 = jnp.bfloat16, jnp.float32
    block = (rows, width)
    several = max(outer - 1, 1)
    dma = pltpu.SemaphoreType.DMA
    anywhere = pl.BlockSpec(memory_space=pl.ANY)
    scratch = [
        pltpu.VMEM((per_index, outer) + block, bf16),
        pltpu.VMEM((per_index, outer) + block, bf16),
        pltpu.VMEM((per_index, several) + block, bf16),
        pltpu.VMEM((per_index, several) + block, bf16),
        pltpu.VMEM((layers, per_index) + block, bf16),
        pltpu.VMEM((layers,) + block, bf16),
        pltpu.VMEM((layers,) + block, bf16),
        pltpu.VMEM((capacity, height, width), bf16),
        pltpu.VMEM((capacity, width, width), bf16),
        pltpu.VMEM(stat_left.shape, f32),
        pltpu.VMEM(stat_right.shape, f32),
        pltpu.VMEM(adam_second.shape, f32),
        pltpu.VMEM(weights.shape, f32),
        pltpu.VMEM(root_left.shape, bf16),
        pltpu.VMEM(weights.shape, f32),
        pltpu.VMEM(weights.shape, bf16),
        pltpu.VMEM((capacity, 8, 128), f32),
        pltpu.VMEM((replicas - 1, capacity, 8, 128), f32),
        dma((6,)),
        dma((per_index, outer)),
        dma((4, capacity)),
        dma((per_index, outer)),
        dma((per_index, outer)),
        dma((per_index, several)),
        dma((per_index, several)),
        dma((layers, per_index)),
        dma((layers, per_index)),
        dma((layers, per_index)),
        dma((layers,)),
        dma((layers,)),
        dma((4, capacity, outer)),
        dma((4, capacity, outer)),
        dma((4, capacity, outer)),
        dma((capacity, replicas - 1)),
        dma((capacity, replicas - 1)),
    ]
    products = 5 * 2 * capacity * rows * width * width
    moved = 2 * grads.size + 32 * weights.size + 2 * capacity * height * width
    return pl.pallas_call(
        functools.partial(kernel, replicas, owners),
        out_shape=(
            jax.ShapeDtypeStruct((capacity, height, width), bf16),
            jax.ShapeDtypeStruct(stat_left.shape, f32),
            jax.ShapeDtypeStruct(stat_right.shape, f32),
            jax.ShapeDtypeStruct(adam_second.shape, f32),
        ),
        in_specs=[pl.BlockSpec(memory_space=pltpu.SMEM)] + [anywhere] * 7,
        out_specs=(anywhere,) * 4,
        scratch_shapes=scratch,
        cost_estimate=pl.CostEstimate(
            flops=products, bytes_accessed=moved, transcendentals=weights.size
        ),
        compiler_params=pltpu.CompilerParams(
            collective_id=0, has_side_effects=True, vmem_limit_bytes=56 * 1024 * 1024
        ),
    )(owner, grads, weights, stat_left, stat_right, adam_second, root_left, root_right)


def solution(mesh):
    placed = (
        P("dp", "own", None, None),
        P(),
        P("own", "dp", None),
        P("own", "dp", None),
        P("own", "dp", None),
        P("own", "dp", None),
        P("own", "dp", None),
        P("own", "dp", None),
    )
    return jax.shard_map(
        functools.partial(on_device, mesh.shape["dp"], mesh.shape["own"]),
        mesh=mesh,
        in_specs=placed,
        out_specs=(
            P("own", None, None),
            P("own", "dp", None),
            P("own", "dp", None),
            P("own", "dp", None),
        ),
        check_vma=False,
    )
```

time: 273 us -> 135 us (0.49)
  waiting for transfers between devices: 215 us -> 0 us
  Pallas kernels: 0 us -> 122 us
  matrix products: 18.2 us -> 0 us
  between operations: 13.9 us -> 0.65 us
  other arithmetic: 8.62 us -> 0 us
  blocking collectives: 5.87 us -> 0 us
    all_gather x4 -> x0, waiting for transfers between devices: 175 us -> none  [the longest x1 81.3 us: on_device(): every = lax.all_gather(summed, 'own', axis=0, tiled=True)]
    pallas_call x0 -> x1, Pallas kernels: none -> 122 us  [on_device(): pl.pallas_call(functools.partial(kernel, replicas, owners), out_shape=(ja...]
    reduce_scatter x1 -> x0, waiting for transfers between devices: 38.4 us -> none  [on_device(): lax.psum_scatter(grads[0].astype(jnp.float32).astype(jnp.bfloat16), 'dp',...]
    dot_general x4 -> x0, matrix products: 18.2 us -> none  [the longest x1 7.19 us: on_device(): jnp.einsum('src,scd->srd', half, lax.all_gather(root_right, 'dp', axis=1,...]
    psum x1 -> x0, blocking collectives: 5.87 us -> none  [on_device(): adam_total, prec_total = lax.psum((adam_sq, prec_sq), 'dp')]
    reduce_sum x2 -> x0, other arithmetic: 4.77 us -> none  [the longest x1 4.59 us: on_device(): adam_sq = jnp.sum(adam_dir * adam_dir, axis=(1, 2))]
    convert_element_type x1 -> x0, other arithmetic: 3.83 us -> none  [on_device(): fresh_rows = (weights - graft[:, None, None] * precond).astype(jnp.bfloat16)]
    unnamed x13 -> x10, local copies, waits for them, and re-layouts: 10.9 us -> 11.4 us
  transfers between devices with their start and end apart: 5 -> 0, of which waited for: 5 -> 0; matrix products, arithmetic and copies ran while one was open for 8% -> 0% of each run, Pallas kernels for 0% -> 0%
where the time goes in v1:
time: 135 us; the launch traced here: 134 us
  Pallas kernels  122 us (90%)
  local copies, waits for them, and re-layouts  11.4 us (8%)
    pallas_call x1, Pallas kernels, on_device(): pl.pallas_call(functools.partial(kernel, replicas, owners), out_shape=(ja...  122 us
    unnamed x10, local copies, waits for them, and re-layouts  11.4 us

profile of v1, /device:TPU:0, one launch (start us, length us, event | category | flops | bytes accessed | tf_op | source)
XLA Modules:
  0.0 134.4 jit_solution(15846556451064590775)
XLA Ops:
  0.6 122.3 %shard_map.111 = (bf16[4,768,768]{2,1,0:T(8,128)(2,1)}, f32[4,192,768]{2,1,0:T(8,128)}, f32[4,192,768]{2,1,0:T(8,128)}, f32[4,192,768]{2,1,0:T(8,128)}) custom-call(s32[16]{0:T(128)} %owner_ref.1, bf16[1,2,768,768]{3,2,1,0:T(8,128)(2,1)} %grads.1, f32[4,192,768]{2,1,0:T(8,128)} %weights.1, f32[4,192,768]{2,1,0:T(8,128)} %stat_left.1, ...), custom_call_target="tpu_custom_call" | custom-call | flops 4529848320 | bytes 25952256 | tf_op jit(solution)/shard_map/pallas_call | solution.py:504
  123.0 0.0 copy-start.2
  123.0 5.0 %copy.16 = bf16[4,768,768]{2,1,0:T(8,128)(2,1)} copy(bf16[4,768,768]{2,1,0:T(8,128)(2,1)} %get-tuple-element.8) | data formatting | bytes 9437184
  128.0 0.0 copy-done.2
  128.0 0.0 copy-start.1
  128.0 1.4 %copy.17 = f32[4,192,768]{2,1,0:T(8,128)} copy(f32[4,192,768]{2,1,0:T(8,128)S(1)} %copy-done.2) | data formatting | bytes 4718592
  129.4 1.1 copy-done.1
  130.5 0.0 copy-start
  130.5 1.4 %copy.18 = f32[4,192,768]{2,1,0:T(8,128)} copy(f32[4,192,768]{2,1,0:T(8,128)S(1)} %copy-done.1) | data formatting | bytes 4718592
  131.9 1.1 copy-done
  133.0 1.4 %copy.19 = f32[4,192,768]{2,1,0:T(8,128)} copy(f32[4,192,768]{2,1,0:T(8,128)S(1)} %copy-done) | data formatting | bytes 4718592
Async XLA Ops:
  123.0 5.0 %copy-start.2 = (f32[4,192,768]{2,1,0:T(8,128)S(1)}, f32[4,192,768]{2,1,0:T(8,128)}, u32[]{:S(2)}) copy-start(f32[4,192,768]{2,1,0:T(8,128)} %get-tuple-element.9) | copy-start | bytes 7077892
  128.0 2.5 %copy-start.1 = (f32[4,192,768]{2,1,0:T(8,128)S(1)}, f32[4,192,768]{2,1,0:T(8,128)}, u32[]{:S(2)}) copy-start(f32[4,192,768]{2,1,0:T(8,128)} %get-tuple-element.10) | copy-start | bytes 7077892
  130.5 2.5 %copy-start = (f32[4,192,768]{2,1,0:T(8,128)S(1)}, f32[4,192,768]{2,1,0:T(8,128)}, u32[]{:S(2)}) copy-start(f32[4,192,768]{2,1,0:T(8,128)} %get-tuple-element.11) | copy-start | bytes 7077892

commit v2 on v1

--- a/solution.py
+++ b/solution.py
@@ -9,6 +9,7 @@
 
 MESH = pl.DeviceIdType.MESH
 PAIR = 2
+CHUNK = 256
 
 
 def dot(a, b):
@@ -76,6 +77,7 @@
     count = per_index * owners
     capacity = weights.shape[0]
     rows = weights.shape[1]
+    chunks = weights.shape[2] // CHUNK
     me = lax.axis_index("dp")
     mine = lax.axis_index("own")
     y, c = lax.div(me, PAIR), lax.rem(me, PAIR)
@@ -90,6 +92,9 @@
 
     def span(yy, cc):
         return pl.ds(pl.multiple_of((yy * PAIR + cc) * rows, rows), rows)
+
+    def part(q):
+        return pl.ds(q * CHUNK, CHUNK)
 
     def shifted(k):
         return lax.rem(y + k, outer)
@@ -115,7 +120,7 @@
     for b in range(per_index):
         for k in range(outer):
             copy = pltpu.make_async_copy(
-                grads.at[0, b, span(shifted(k), c)], own_rows.at[b, k], own_sem.at[b, k]
+                grads.at[0, b, span(shifted(k), c)], own_rows.at[k, b], own_sem.at[b, k]
             )
             copy.start()
             own_copies[b, k] = copy
@@ -143,11 +148,11 @@
 
     order = list(range(1, outer)) + [0]
     core_copies = {}
-    for b in range(per_index):
-        for k in order:
+    for k in order:
+        for b in range(per_index):
             copy = remote(
                 grads.at[0, b, span(shifted(k), 1 - c)],
-                core_in.at[b, k],
+                core_in.at[k, b],
                 core_s.at[b, k],
                 core_r.at[b, k],
                 core_peer,
@@ -166,23 +171,26 @@
     for copy in loads:
         copy.start()
 
-    part_copies = []
-    for b in range(per_index):
+    def part_copy(q, k):
+        return remote(
+            part_out.at[q, k - 1],
+            part_in.at[q, k - 1],
+            part_s.at[q, k - 1],
+            part_r.at[q, k - 1],
+            replica(shifted(k), c),
+        )
+
+    def chip_sum(q, k):
+        return own_rows[k, :, :, part(q)].astype(f32) + core_in[k, :, :, part(q)].astype(f32)
+
+    for q in range(chunks):
         for k in range(1, outer):
-            own_copies[b, k].wait()
-            core_copies[b, k].wait_recv()
-            part_out[b, k - 1] = (
-                own_rows[b, k].astype(f32) + core_in[b, k].astype(f32)
-            ).astype(bf16)
-            copy = remote(
-                part_out.at[b, k - 1],
-                part_in.at[b, k - 1],
-                part_s.at[b, k - 1],
-                part_r.at[b, k - 1],
-                replica(shifted(k), c),
-            )
-            copy.start()
-            part_copies.append(copy)
+            if q == 0:
+                for b in range(per_index):
+                    own_copies[b, k].wait()
+                    core_copies[b, k].wait_recv()
+            part_out[q, k - 1] = chip_sum(q, k).astype(bf16)
+            part_copy(q, k).start()
 
     def far_copy(src, ref, s, k, sems):
         return remote(
@@ -226,99 +234,94 @@
     loads[0].wait()
     slots(lambda s: gather_start(roots.at[s, span(y, c)], roots, s, root_sems))
 
-    def send_up(src, k, b):
+    def send_up(src, d, q):
         return remote(
-            blocks.at[src, b],
-            blocks.at[src, b],
-            up_s.at[k, b],
-            block_r.at[src, b],
+            blocks.at[src, q],
+            blocks.at[src, q],
+            up_s.at[d, q],
+            block_r.at[src, q],
             group(o + 1, i),
         )
 
-    def send_down(src, k, b):
+    def send_down(src, d, q):
         return remote(
-            blocks.at[src, b],
-            blocks.at[src, b],
-            down_s.at[k, b],
-            block_r.at[src, b],
+            blocks.at[src, q],
+            blocks.at[src, q],
+            down_s.at[d, q],
+            block_r.at[src, q],
             group(o - 1, i),
         )
 
-    def wait_block(src, b):
+    def wait_block(src, q):
         remote(
-            blocks.at[src, b], blocks.at[src, b], up_s.at[0, b], block_r.at[src, b], cross_peer
+            blocks.at[src, q], blocks.at[src, q], up_s.at[0, q], block_r.at[src, q], cross_peer
         ).wait_recv()
 
-    def cross_copy(src):
+    def cross_copy(src, q):
         return remote(
-            cross_out.at[src], cross_in.at[src], cross_s.at[src], cross_r.at[src], cross_peer
-        )
-
-    def cross(src):
+            cross_out.at[src, q],
+            cross_in.at[src, q],
+            cross_s.at[src, q],
+            cross_r.at[src, q],
+            cross_peer,
+        )
+
+    def cross(src, q):
         first = (src * PAIR + i) * per_index
         other = o * PAIR + 1 - i
-        sent = blocks[src, 0]
+        sent = blocks[src, q, 0]
         for b in range(1, per_index):
-            sent = jnp.where(owner_ref[first + b] == other, blocks[src, b], sent)
-        cross_out[src] = sent
-        cross_copy(src).start()
-
-    for b in range(per_index):
-        own_copies[b, 0].wait()
-        core_copies[b, 0].wait_recv()
-        total = own_rows[b, 0].astype(f32) + core_in[b, 0].astype(f32)
+            sent = jnp.where(owner_ref[first + b] == other, blocks[src, q, b], sent)
+        cross_out[src, q] = sent
+        cross_copy(src, q).start()
+
+    def own_total(q):
+        if q == 0:
+            for b in range(per_index):
+                own_copies[b, 0].wait()
+                core_copies[b, 0].wait_recv()
+        total = chip_sum(q, 0)
         for k in range(1, outer):
-            remote(
-                part_out.at[b, k - 1],
-                part_in.at[b, k - 1],
-                part_s.at[b, k - 1],
-                part_r.at[b, k - 1],
-                core_peer,
-            ).wait_recv()
-            total = total + part_in[b, k - 1].astype(f32)
-        blocks[o, b] = total.astype(bf16)
+            part_copy(q, k).wait_recv()
+            total = total + part_in[q, k - 1].astype(f32)
+        blocks[o, q] = total.astype(bf16)
 
         @pl.when(above)
         def _():
-            send_up(o, 0, b).start()
+            send_up(o, 0, q).start()
 
         @pl.when(below)
         def _():
-            send_down(o, 0, b).start()
-
-    cross(o)
-    for d in range(1, layers):
-        for b in range(per_index):
-
-            @pl.when(o >= d)
+            send_down(o, 0, q).start()
+
+        cross(o, q)
+
+    def pass_on(d, q):
+        @pl.when(o >= d)
+        def _():
+            wait_block(o - d, q)
+
+            @pl.when(above)
             def _():
-                wait_block(o - d, b)
-
-                @pl.when(above)
-                def _():
-                    send_up(o - d, d, b).start()
-
-            @pl.when(o + d < layers)
+                send_up(o - d, d, q).start()
+
+        @pl.when(o + d < layers)
+        def _():
+            wait_block(o + d, q)
+
+            @pl.when(below)
             def _():
-                wait_block(o + d, b)
-
-                @pl.when(below)
-                def _():
-                    send_down(o + d, d, b).start()
+                send_down(o + d, d, q).start()
 
         @pl.when(o >= d)
         def _():
-            cross(o - d)
+            cross(o - d, q)
 
         @pl.when(o + d < layers)
         def _():
-            cross(o + d)
-
-    slots(lambda s: gather_forward(roots, s, root_sems))
-    for src in range(layers):
-        cross_copy(src).wait_recv()
-
-    def choose(s):
+            cross(o + d, q)
+
+    def choose(q, s):
         found = jnp.int32(0)
         seen = jnp.int32(0)
         valid = jnp.int32(0)
@@ -330,13 +333,32 @@
             seen = seen + hit
         source = lax.div(found, per_index)
         layer, side = lax.div(source, PAIR), lax.rem(source, PAIR)
-        straight = blocks[layer, lax.rem(found, per_index)]
-        crossed = cross_in[layer]
-        picked = jnp.where(side == i, straight, crossed)
-        full[s, span(y, c)] = jnp.where(valid == 1, picked, jnp.zeros_like(picked))
-        gather_start(full.at[s, span(y, c)], full, s, grad_sems)
-
-    slots(choose)
+        within = lax.rem(found, per_index)
+        crossed = jnp.zeros_like(cross_in[0, q])
+        for src in range(layers):
+            taken = cross_in[src, q]
+            for b in range(per_index):
+                straight = blocks[src, q, b]
+                taken = jnp.where((side == i) & (within == b), straight, taken)
+            crossed = jnp.where((layer == src) & (valid == 1), taken, crossed)
+        f = q * capacity + s
+        full[f, span(y, c)] = crossed
+        gather_start(full.at[f, span(y, c)], full, f, grad_sems)
+
+    def choose_chunk(q):
+        for src in range(layers):
+            cross_copy(src, q).wait_recv()
+        slots(functools.partial(choose, q))
+
+    for t in range(chunks + layers):
+        if 0 <= t - layers < chunks:
+            choose_chunk(t - layers)
+        for d in range(layers - 1, 0, -1):
+            if 0 <= t - d < chunks:
+                pass_on(d, t - d)
+        if t < chunks:
+            own_total(t)
+
     for copy in loads[1:]:
         copy.wait()
 
@@ -358,6 +380,37 @@
         return pltpu.make_async_copy(
             fresh.at[s], out_weights.at[s, span(y, c)], store_sem.at[3, s]
         )
+
+    def moments(s):
+        adam_sq = jnp.float32(0)
+        for q in range(chunks):
+            grad32 = full[q * capacity + s, span(y, c)].astype(f32)
+            second = 0.9 * second_v[s, :, part(q)] + 0.1 * grad32 * grad32
+            second_v[s, :, part(q)] = second
+            direction = grad32 / (jnp.sqrt(second) + 1e-08)
+            adam_sq = adam_sq + jnp.sum(direction * direction)
+        norm_out[s] = jnp.where(row_of < 4, adam_sq, 0.0)
+        store(second_v, out_second, 0, s).start()
+
+    def product(q, s):
+        f = q * capacity + s
+        gather_arrived(full, f, grad_sems)
+        half = dot(root_v[s], full[f]).astype(bf16)
+        return dot(half, roots[s, part(q), :])
+
+    def accumulate(q, s):
+        if q == 0:
+            gather_arrived(roots, s, root_sems)
+            precond[s] = product(q, s)
+        else:
+            precond[s] = precond[s] + product(q, s)
+
+    def precondition(s):
+        accumulate(chunks - 1, s)
+        result = precond[s]
+        norm_out[s] = norm_out[s] + jnp.where(row_of < 4, 0.0, jnp.sum(result * result))
+        for k in range(1, replicas):
+            norm_copy(s, k).start()
 
     def update(s):
         norms = norm_out[s]
@@ -369,67 +422,79 @@
         gather_start(fresh.at[s], out_weights, s, weight_sems)
         own_output(s).start()
 
-    def precondition(s):
-        grad32 = full[s, span(y, c)].astype(f32)
-        second = 0.9 * second_v[s] + 0.1 * grad32 * grad32
-        second_v[s] = second
-        store(second_v, out_second, 0, s).start()
-        direction = grad32 / (jnp.sqrt(second) + 1e-08)
-        adam_sq = jnp.sum(direction * direction)
-        gather_forward(full, s, grad_sems)
-        gather_arrived(full, s, grad_sems)
-        gather_arrived(roots, s, root_sems)
-        half = dot(root_v[s], full[s]).astype(bf16)
-        result = dot(half, roots[s])
-        precond[s] = result
-        norm_out[s] = jnp.where(row_of < 4, adam_sq, jnp.sum(result * result))
-        for k in range(1, replicas):
-            norm_copy(s, k).start()
-
-        @pl.when(s >= 1)
-        def _():
-            update(s - 1)
-
-    slots(precondition)
-    update(capacity - 1)
-
-    width = full.shape[2]
+    slots(moments)
+    slots(lambda s: gather_forward(roots, s, root_sems))
+    for q in range(chunks - 1):
+        slots(lambda s: gather_forward(full, q * capacity + s, grad_sems))
+        slots(functools.partial(accumulate, q))
+
+    def last(s, carry):
+        @pl.when(s < capacity)
+        def _():
+            gather_forward(full, (chunks - 1) * capacity + s, grad_sems)
+
+        @pl.when((s >= 1) & (s <= capacity))
+        def _():
+            precondition(s - 1)
+
+        @pl.when(s >= 2)
+        def _():
+            update(s - 2)
+
+        return carry
+
+    lax.fori_loop(0, capacity + 2, last, 0)
+
+    width = weights.shape[2]
     cols = width // replicas
-    shape = (cols, width)
-    pick = (
-        lax.broadcasted_iota(jnp.int32, shape, 1)
-        == lax.broadcasted_iota(jnp.int32, shape, 0) + me * cols
-    ).astype(f32).astype(bf16)
+
+    def pick(q):
+        shape = (cols, CHUNK)
+        column = lax.broadcasted_iota(jnp.int32, shape, 1) + q * CHUNK
+        wanted = lax.broadcasted_iota(jnp.int32, shape, 0) + me * cols
+        return (column == wanted).astype(f32).astype(bf16)
 
     def statistics(s):
-        left_v[s] = 0.5 * left_v[s] + 0.5 * dot_nt(full[s, span(y, c)], full[s])
+        left, columns = 0.0, 0.0
+        for q in range(chunks):
+            f = q * capacity + s
+            left = left + dot_nt(full[f, span(y, c)], full[f])
+            columns = columns + dot_nt(pick(q), full[f])
+        left_v[s] = 0.5 * left_v[s] + 0.5 * left
         store(left_v, out_left, 1, s).start()
-        columns = dot_nt(pick, full[s]).astype(bf16)
-        right_v[s] = 0.5 * right_v[s] + 0.5 * dot(columns, full[s])
+        columns = columns.astype(bf16)
+        for q in range(chunks):
+            right_v[s, :, part(q)] = 0.5 * right_v[s, :, part(q)] + 0.5 * dot(
+                columns, full[q * capacity + s]
+            )
         store(right_v, out_right, 2, s).start()
         gather_forward(out_weights, s, weight_sems)
 
     slots(statistics)
 
-    for copy in list(core_copies.values()) + part_copies:
+    for copy in core_copies.values():
         copy.wait_send()
-    for k in range(layers - 1):
-        for b in range(per_index):
-
-            @pl.when(above & (o >= k))
+    for q in range(chunks):
+        for k in range(1, outer):
+            part_copy(q, k).wait_send()
+        for d in range(layers - 1):
+
+            @pl.when(above & (o >= d))
             def _():
-                send_up(o - k, k, b).wait_send()
-
-            @pl.when(below & (o + k < layers))
+                send_up(o - d, d, q).wait_send()
+
+            @pl.when(below & (o + d < layers))
             def _():
-                send_down(o + k, k, b).wait_send()
-
-    for src in range(layers):
-        cross_copy(src).wait_send()
+                send_down(o + d, d, q).wait_send()
+
+        for src in range(layers):
+            cross_copy(src, q).wait_send()
 
     def finish(s):
         gather_sent(roots.at[s, span(y, c)], roots, s, root_sems)
-        gather_sent(full.at[s, span(y, c)], full, s, grad_sems)
+        for q in range(chunks):
+            f = q * capacity + s
+            gather_sent(full.at[f, span(y, c)], full, f, grad_sems)
         for k in range(1, replicas):
             norm_copy(s, k).wait_send()
         store(second_v, out_second, 0, s).wait()
@@ -458,19 +523,20 @@
     per_index, height = grads.shape[1], grads.shape[2]
     outer, layers = replicas // PAIR, owners // PAIR
     bf16, f32 = jnp.bfloat16, jnp.float32
-    block = (rows, width)
+    block, piece = (rows, width), (rows, CHUNK)
+    chunks = width // CHUNK
     several = max(outer - 1, 1)
     dma = pltpu.SemaphoreType.DMA
     anywhere = pl.BlockSpec(memory_space=pl.ANY)
     scratch = [
-        pltpu.VMEM((per_index, outer) + block, bf16),
-        pltpu.VMEM((per_index, outer) + block, bf16),
-        pltpu.VMEM((per_index, several) + block, bf16),
-        pltpu.VMEM((per_index, several) + block, bf16),
-        pltpu.VMEM((layers, per_index) + block, bf16),
-        pltpu.VMEM((layers,) + block, bf16),
-        pltpu.VMEM((layers,) + block, bf16),
-        pltpu.VMEM((capacity, height, width), bf16),
+        pltpu.VMEM((outer, per_index) + block, bf16),
+        pltpu.VMEM((outer, per_index) + block, bf16),
+        pltpu.VMEM((chunks, several, per_index) + piece, bf16),
+        pltpu.VMEM((chunks, several, per_index) + piece, bf16),
+        pltpu.VMEM((layers, chunks, per_index) + piece, bf16),
+        pltpu.VMEM((layers, chunks) + piece, bf16),
+        pltpu.VMEM((layers, chunks) + piece, bf16),
+        pltpu.VMEM((chunks * capacity, height, CHUNK), bf16),
         pltpu.VMEM((capacity, width, width), bf16),
         pltpu.VMEM(stat_left.shape, f32),
         pltpu.VMEM(stat_right.shape, f32),
@@ -486,14 +552,14 @@
         dma((4, capacity)),
         dma((per_index, outer)),
         dma((per_index, outer)),
-        dma((per_index, several)),
-        dma((per_index, several)),
-        dma((layers, per_index)),
-        dma((layers, per_index)),
-        dma((layers, per_index)),
-        dma((layers,)),
-        dma((layers,)),
-        dma((4, capacity, outer)),
+        dma((chunks, several)),
+        dma((chunks, several)),
+        dma((layers, chunks)),
+        dma((layers, chunks)),
+        dma((layers, chunks)),
+        dma((layers, chunks)),
+        dma((layers, chunks)),
+        dma((4, chunks * capacity, outer)),
         dma((4, capacity, outer)),
         dma((4, capacity, outer)),
         dma((capacity, replicas - 1)),
@@ -516,7 +582,7 @@
             flops=products, bytes_accessed=moved, transcendentals=weights.size
         ),
         compiler_params=pltpu.CompilerParams(
-            collective_id=0, has_side_effects=True, vmem_limit_bytes=56 * 1024 * 1024
+            collective_id=0, has_side_effects=True, vmem_limit_bytes=40 * 1024 * 1024
         ),
     )(owner, grads, weights, stat_left, stat_right, adam_second, root_left, root_right)
 

time: 135 us -> 123 us (0.911)
  Pallas kernels: 122 us -> 107 us
  local copies, waits for them, and re-layouts: 11.4 us -> 15.6 us
    pallas_call x1, Pallas kernels: 122 us -> 107 us  [on_device(): pl.pallas_call(functools.partial(kernel, replicas, owners), out_shape=(ja...]
    unnamed x10 -> x14, local copies, waits for them, and re-layouts: 11.4 us -> 15.6 us
where the time goes in v2:
time: 123 us
  Pallas kernels  107 us (87%)
  local copies, waits for them, and re-layouts  15.6 us (13%)
    pallas_call x1, Pallas kernels, on_device(): pl.pallas_call(functools.partial(kernel, replicas, owners), out_shape=(ja...  107 us
    unnamed x14, local copies, waits for them, and re-layouts  15.6 us

profile of v2, /device:TPU:0, one launch (start us, length us, event | category | flops | bytes accessed | tf_op | source)
XLA Modules:
  0.0 122.8 jit_solution(7332384753843279476)
XLA Ops:
  0.6 0.0 copy-start
  0.6 1.7 %copy-done = bf16[1,2,768,768]{3,2,1,0:T(8,128)(2,1)S(1)} copy-done((bf16[1,2,768,768]{3,2,1,0:T(8,128)(2,1)S(1)}, bf16[1,2,768,768]{3,2,1,0:T(8,128)(2,1)}, u32[]{:S(2)}) %copy-start) | copy-done | bytes 2359320
  2.3 0.0 copy-start.1
  2.3 1.7 %copy-done.1 = f32[4,192,768]{2,1,0:T(8,128)S(1)} copy-done((f32[4,192,768]{2,1,0:T(8,128)S(1)}, f32[4,192,768]{2,1,0:T(8,128)}, u32[]{:S(2)}) %copy-start.1) | copy-done | bytes 2359320
  4.0 0.0 copy-start.2
  4.0 1.3 %copy-done.2 = bf16[4,192,768]{2,1,0:T(8,128)(2,1)S(1)} copy-done((bf16[4,192,768]{2,1,0:T(8,128)(2,1)S(1)}, bf16[4,192,768]{2,1,0:T(8,128)(2,1)}, u32[]{:S(2)}) %copy-start.2) | copy-done | bytes 1179672
  5.2 0.0 copy-start.3
  5.2 1.3 %copy-done.3 = bf16[4,192,768]{2,1,0:T(8,128)(2,1)S(1)} copy-done((bf16[4,192,768]{2,1,0:T(8,128)(2,1)S(1)}, bf16[4,192,768]{2,1,0:T(8,128)(2,1)}, u32[]{:S(2)}) %copy-start.3) | copy-done | bytes 1179672
  6.5 0.0 copy-start.4
  6.5 0.7 copy-done.4
  7.2 106.6 %shard_map.111 = (bf16[4,768,768]{2,1,0:T(8,128)(2,1)}, f32[4,192,768]{2,1,0:T(8,128)S(1)}, f32[4,192,768]{2,1,0:T(8,128)S(1)}, f32[4,192,768]{2,1,0:T(8,128)S(1)}) custom-call(s32[16]{0:T(128)S(1)} %copy-done.4, bf16[1,2,768,768]{3,2,1,0:T(8,128)(2,1)S(1)} %copy-done, f32[4,192,768]{2,1,0:T(8,128)S(1)} %copy-done.1, f32[4,192,768]{2,1,0:T(8,128)} %stat_left.1, ...), custom_call_target="tpu_custom_call" | custom-call | flops 4529848320 | bytes 25952256 | tf_op jit(solution)/shard_map/pallas_call | solution.py:570
  113.8 4.8 %copy.16 = bf16[4,768,768]{2,1,0:T(8,128)(2,1)} copy(bf16[4,768,768]{2,1,0:T(8,128)(2,1)} %get-tuple-element.8) | data formatting | bytes 9437184
  118.6 1.4 %copy.17 = f32[4,192,768]{2,1,0:T(8,128)} copy(f32[4,192,768]{2,1,0:T(8,128)S(1)} %get-tuple-element.9) | data formatting | bytes 4718592
  120.0 1.4 %copy.18 = f32[4,192,768]{2,1,0:T(8,128)} copy(f32[4,192,768]{2,1,0:T(8,128)S(1)} %get-tuple-element.10) | data formatting | bytes 4718592
  121.4 1.4 %copy.19 = f32[4,192,768]{2,1,0:T(8,128)} copy(f32[4,192,768]{2,1,0:T(8,128)S(1)} %get-tuple-element.11) | data formatting | bytes 4718592
Async XLA Ops:
  0.6 1.7 %copy-start = (bf16[1,2,768,768]{3,2,1,0:T(8,128)(2,1)S(1)}, bf16[1,2,768,768]{3,2,1,0:T(8,128)(2,1)}, u32[]{:S(2)}) copy-start(bf16[1,2,768,768]{3,2,1,0:T(8,128)(2,1)} %grads.1) | copy-start | bytes 7077892
  2.3 1.7 %copy-start.1 = (f32[4,192,768]{2,1,0:T(8,128)S(1)}, f32[4,192,768]{2,1,0:T(8,128)}, u32[]{:S(2)}) copy-start(f32[4,192,768]{2,1,0:T(8,128)} %weights.1) | copy-start | bytes 7077892
  4.0 1.3 %copy-start.2 = (bf16[4,192,768]{2,1,0:T(8,128)(2,1)S(1)}, bf16[4,192,768]{2,1,0:T(8,128)(2,1)}, u32[]{:S(2)}) copy-start(bf16[4,192,768]{2,1,0:T(8,128)(2,1)} %root_left.1) | copy-start | bytes 3538948
  5.2 1.3 %copy-start.3 = (bf16[4,192,768]{2,1,0:T(8,128)(2,1)S(1)}, bf16[4,192,768]{2,1,0:T(8,128)(2,1)}, u32[]{:S(2)}) copy-start(bf16[4,192,768]{2,1,0:T(8,128)(2,1)} %root_right.1) | copy-start | bytes 3538948
  6.5 0.7 copy-start.4

commit v3 on v2

--- a/solution.py
+++ b/solution.py
@@ -507,6 +507,19 @@
     slots(finish)
 
 
+def write_out(*refs):
+    sources, targets, sems = refs[:4], refs[4:8], refs[8]
+    copies = [
+        pltpu.make_async_copy(source.at[s], target.at[s], sems.at[n, s])
+        for n, (source, target) in enumerate(zip(sources, targets))
+        for s in range(source.shape[0])
+    ]
+    for copy in copies:
+        copy.start()
+    for copy in copies:
+        copy.wait()
+
+
 def on_device(
     replicas,
     owners,
@@ -567,14 +580,21 @@
     ]
     products = 5 * 2 * capacity * rows * width * width
     moved = 2 * grads.size + 32 * weights.size + 2 * capacity * height * width
-    return pl.pallas_call(
+    results = (
+        ((capacity, height, width), bf16),
+        (stat_left.shape, f32),
+        (stat_right.shape, f32),
+        (adam_second.shape, f32),
+    )
+    arrays = [
+        pltpu.with_memory_space_constraint(array, pltpu.HBM)
+        for array in (
+            grads, weights, stat_left, stat_right, adam_second, root_left, root_right
+        )
+    ]
+    near = pl.pallas_call(
         functools.partial(kernel, replicas, owners),
-        out_shape=(
-            jax.ShapeDtypeStruct((capacity, height, width), bf16),
-            jax.ShapeDtypeStruct(stat_left.shape, f32),
-            jax.ShapeDtypeStruct(stat_right.shape, f32),
-            jax.ShapeDtypeStruct(adam_second.shape, f32),
-        ),
+        out_shape=tuple(pltpu.VMEM(shape, dtype) for shape, dtype in results),
         in_specs=[pl.BlockSpec(memory_space=pltpu.SMEM)] + [anywhere] * 7,
         out_specs=(anywhere,) * 4,
         scratch_shapes=scratch,
@@ -582,9 +602,16 @@
             flops=products, bytes_accessed=moved, transcendentals=weights.size
         ),
         compiler_params=pltpu.CompilerParams(
-            collective_id=0, has_side_effects=True, vmem_limit_bytes=40 * 1024 * 1024
+            collective_id=0, has_side_effects=True, vmem_limit_bytes=42 * 1024 * 1024
         ),
-    )(owner, grads, weights, stat_left, stat_right, adam_second, root_left, root_right)
+    )(owner, *arrays)
+    return pl.pallas_call(
+        write_out,
+        out_shape=tuple(pltpu.HBM(shape, dtype) for shape, dtype in results),
+        in_specs=[anywhere] * 4,
+        out_specs=(anywhere,) * 4,
+        scratch_shapes=[dma((4, capacity))],
+    )(*near)
 
 
 def solution(mesh):

time: 123 us -> 473 us (3.85)
  Pallas kernels: 107 us -> 465 us
  local copies, waits for them, and re-layouts: 15.6 us -> 7.04 us
    pallas_call x1 -> x2, Pallas kernels: 107 us -> 465 us  [the longest x1 359 us: on_device(): pl.pallas_call(write_out, out_shape=tuple((pltpu.HBM(shape, dtype) for sh...]
    unnamed x14 -> x10, local copies, waits for them, and re-layouts: 15.6 us -> 7.04 us
where the time goes in v3:
time: 473 us; the launch traced here: 472 us
  Pallas kernels  465 us (98%)
  local copies, waits for them, and re-layouts  7.04 us (1%)
    pallas_call x1, Pallas kernels, on_device(): pl.pallas_call(write_out, out_shape=tuple((pltpu.HBM(shape, dtype) for sh...  359 us
    pallas_call x1, Pallas kernels, on_device(): pl.pallas_call(functools.partial(kernel, replicas, owners), out_shape=tup...  106 us

profile of v3, /device:TPU:0, one launch (start us, length us, event | category | flops | bytes accessed | tf_op | source)
XLA Modules:
  0.0 472.4 jit_solution(15083022019039206326)
XLA Ops:
  0.6 0.0 copy-start.4
  0.6 0.6 copy-done.4
  1.3 106.1 %shard_map.111 = (bf16[4,768,768]{2,1,0:T(8,128)(2,1)S(1)}, f32[4,192,768]{2,1,0:T(8,128)S(1)}, f32[4,192,768]{2,1,0:T(8,128)S(1)}, f32[4,192,768]{2,1,0:T(8,128)S(1)}) custom-call(s32[16]{0:T(128)S(1)} %copy-done.4, bf16[1,2,768,768]{3,2,1,0:T(8,128)(2,1)} %grads.1, f32[4,192,768]{2,1,0:T(8,128)} %weights.1, f32[4,192,768]{2,1,0:T(8,128)} %stat_left.1, ...), custom_call_target="tpu_custom_call" | custom-call | flops 4529848320 | bytes 25952256 | tf_op jit(solution)/shard_map/pallas_call | solution.py:595
  107.4 0.0 copy-start
  107.4 2.1 copy-done
  109.6 0.0 copy-start.1
  109.6 1.4 copy-done.1
  111.0 0.0 copy-start.2
  111.0 1.5 copy-done.2
  112.4 0.0 copy-start.3
  112.4 1.4 copy-done.3
  113.8 358.6 %shard_map.112 = (bf16[4,768,768]{2,1,0:T(8,128)(2,1)}, f32[4,192,768]{2,1,0:T(8,128)}, f32[4,192,768]{2,1,0:T(8,128)}, f32[4,192,768]{2,1,0:T(8,128)}) custom-call(bf16[4,768,768]{2,1,0:T(8,128)(2,1)} %copy-done, f32[4,192,768]{2,1,0:T(8,128)} %copy-done.1, f32[4,192,768]{2,1,0:T(8,128)} %copy-done.2, f32[4,192,768]{2,1,0:T(8,128)} %copy-done.3), custom_call_target="tpu_custom_call" | custom-call | tf_op jit(solution)/shard_map/pallas_call | solution.py:608
Async XLA Ops:
  0.6 0.7 copy-start.4
  107.4 2.1 copy-start
  109.6 1.4 copy-start.1
  111.0 1.5 copy-start.2
  112.4 1.4 copy-start.3

commit v4 on v3

--- a/solution.py
+++ b/solution.py
@@ -146,6 +146,45 @@
     lines = above.astype(jnp.int32) + below.astype(jnp.int32)
     pl.semaphore_wait(barrier, replicas + lines)
 
+    def far_copy(src, ref, s, k, sems):
+        return remote(
+            src, ref.at[s, span(y, c)], sems.at[0, s, k], sems.at[1, s, k], replica(shifted(k), c)
+        )
+
+    def near_copy(src, ref, s, k, sems):
+        return remote(
+            src, ref.at[s, span(back(k), c)], sems.at[2, s, k], sems.at[3, s, k], core_peer
+        )
+
+    def gather_start(src, ref, s, sems):
+        for k in range(1, outer):
+            far_copy(src, ref, s, k, sems).start()
+        near_copy(src, ref, s, 0, sems).start()
+
+    def gather_forward(ref, s, sems):
+        for k in range(1, outer):
+            landed = ref.at[s, span(back(k), c)]
+            remote(landed, landed, sems.at[0, s, k], sems.at[1, s, k], core_peer).wait_recv()
+            near_copy(landed, ref, s, k, sems).start()
+
+    def gather_arrived(ref, s, sems):
+        for k in range(outer):
+            landed = ref.at[s, span(back(k), 1 - c)]
+            remote(landed, landed, sems.at[2, s, k], sems.at[3, s, k], core_peer).wait_recv()
+
+    def gather_sent(src, ref, s, sems):
+        for k in range(1, outer):
+            far_copy(src, ref, s, k, sems).wait_send()
+        for k in range(outer):
+            near_copy(src, ref, s, k, sems).wait_send()
+
+    late = capacity - 1
+
+    def roots_start(s):
+        gather_start(root_right.at[s], roots, s, root_sems)
+
+    roots_start(0)
+
     order = list(range(1, outer)) + [0]
     core_copies = {}
     for k in order:
@@ -192,38 +231,6 @@
             part_out[q, k - 1] = chip_sum(q, k).astype(bf16)
             part_copy(q, k).start()
 
-    def far_copy(src, ref, s, k, sems):
-        return remote(
-            src, ref.at[s, span(y, c)], sems.at[0, s, k], sems.at[1, s, k], replica(shifted(k), c)
-        )
-
-    def near_copy(src, ref, s, k, sems):
-        return remote(
-            src, ref.at[s, span(back(k), c)], sems.at[2, s, k], sems.at[3, s, k], core_peer
-        )
-
-    def gather_start(src, ref, s, sems):
-        for k in range(1, outer):
-            far_copy(src, ref, s, k, sems).start()
-        near_copy(src, ref, s, 0, sems).start()
-
-    def gather_forward(ref, s, sems):
-        for k in range(1, outer):
-            landed = ref.at[s, span(back(k), c)]
-            remote(landed, landed, sems.at[0, s, k], sems.at[1, s, k], core_peer).wait_recv()
-            near_copy(landed, ref, s, k, sems).start()
-
-    def gather_arrived(ref, s, sems):
-        for k in range(outer):
-            landed = ref.at[s, span(back(k), 1 - c)]
-            remote(landed, landed, sems.at[2, s, k], sems.at[3, s, k], core_peer).wait_recv()
-
-    def gather_sent(src, ref, s, sems):
-        for k in range(1, outer):
-            far_copy(src, ref, s, k, sems).wait_send()
-        for k in range(outer):
-            near_copy(src, ref, s, k, sems).wait_send()
-
     def slots(body):
         def step(s, carry):
             body(s)
@@ -231,8 +238,8 @@
 
         lax.fori_loop(0, capacity, step, 0)
 
-    loads[0].wait()
-    slots(lambda s: gather_start(roots.at[s, span(y, c)], roots, s, root_sems))
+    for s in range(1, late):
+        roots_start(s)
 
     def send_up(src, d, q):
         return remote(
@@ -359,7 +366,7 @@
         if t < chunks:
             own_total(t)
 
-    for copy in loads[1:]:
+    for copy in loads:
         copy.wait()
 
     def store(ref, out, which, s):
@@ -422,28 +429,42 @@
         gather_start(fresh.at[s], out_weights, s, weight_sems)
         own_output(s).start()
 
+    def early(body):
+        def step(s, carry):
+            body(s)
+            return carry
+
+        lax.fori_loop(0, late, step, 0)
+
     slots(moments)
-    slots(lambda s: gather_forward(roots, s, root_sems))
+    early(lambda s: gather_forward(roots, s, root_sems))
     for q in range(chunks - 1):
         slots(lambda s: gather_forward(full, q * capacity + s, grad_sems))
-        slots(functools.partial(accumulate, q))
+        early(functools.partial(accumulate, q))
 
     def last(s, carry):
-        @pl.when(s < capacity)
-        def _():
-            gather_forward(full, (chunks - 1) * capacity + s, grad_sems)
-
-        @pl.when((s >= 1) & (s <= capacity))
+        gather_forward(full, (chunks - 1) * capacity + s, grad_sems)
+
+        @pl.when(s >= 1)
         def _():
             precondition(s - 1)
 
+        @pl.when(s == 1)
+        def _():
+            roots_start(late)
+
         @pl.when(s >= 2)
         def _():
             update(s - 2)
 
         return carry
 
-    lax.fori_loop(0, capacity + 2, last, 0)
+    lax.fori_loop(0, capacity, last, 0)
+    gather_forward(roots, late, root_sems)
+    for q in range(chunks - 1):
+        accumulate(q, late)
+    precondition(late)
+    update(late - 1)
 
     width = weights.shape[2]
     cols = width // replicas
@@ -468,9 +489,12 @@
                 columns, full[q * capacity + s]
             )
         store(right_v, out_right, 2, s).start()
+
+    slots(statistics)
+    gather_forward(out_weights, 0, weight_sems)
+    update(late)
+    for s in range(1, capacity):
         gather_forward(out_weights, s, weight_sems)
-
-    slots(statistics)
 
     for copy in core_copies.values():
         copy.wait_send()
@@ -604,14 +628,15 @@
         compiler_params=pltpu.CompilerParams(
             collective_id=0, has_side_effects=True, vmem_limit_bytes=42 * 1024 * 1024
         ),
-    )(owner, *arrays)
+    )(pltpu.with_memory_space_constraint(owner, pltpu.HBM), *arrays)
     return pl.pallas_call(
         write_out,
         out_shape=tuple(pltpu.HBM(shape, dtype) for shape, dtype in results),
         in_specs=[anywhere] * 4,
         out_specs=(anywhere,) * 4,
         scratch_shapes=[dma((4, capacity))],
-    )(*near)
+        compiler_params=pltpu.CompilerParams(vmem_limit_bytes=4 * 1024 * 1024),
+    )(*[pltpu.with_memory_space_constraint(array, pltpu.VMEM) for array in near])
 
 
 def solution(mesh):

time: 473 us -> 115 us (0.24)
  Pallas kernels: 465 us -> 115 us
  local copies, waits for them, and re-layouts: 7.04 us -> 0 us
    pallas_call x1, Pallas kernels: 359 us -> 4.46 us  [on_device(): pl.pallas_call(write_out, out_shape=tuple((pltpu.HBM(shape, dtype) for sh...]
    unnamed x10 -> x0, local copies, waits for them, and re-layouts: 7.04 us -> none
where the time goes in v4:
time: 115 us
  Pallas kernels  115 us (100%)
    pallas_call x1, Pallas kernels, on_device(): pl.pallas_call(functools.partial(kernel, replicas, owners), out_shape=tup...  110 us
    pallas_call x1, Pallas kernels, on_device(): pl.pallas_call(write_out, out_shape=tuple((pltpu.HBM(shape, dtype) for sh...  4.46 us

profile of v4, /device:TPU:0, one launch (start us, length us, event | category | flops | bytes accessed | tf_op | source)
XLA Modules:
  0.0 115.2 jit_solution(14592042320489466775)
XLA Ops:
  0.6 110.1 %shard_map.111 = (bf16[4,768,768]{2,1,0:T(8,128)(2,1)S(1)}, f32[4,192,768]{2,1,0:T(8,128)S(1)}, f32[4,192,768]{2,1,0:T(8,128)S(1)}, f32[4,192,768]{2,1,0:T(8,128)S(1)}) custom-call(s32[16]{0:T(128)} %owner_ref.1, bf16[1,2,768,768]{3,2,1,0:T(8,128)(2,1)} %grads.1, f32[4,192,768]{2,1,0:T(8,128)} %weights.1, f32[4,192,768]{2,1,0:T(8,128)} %stat_left.1, ...), custom_call_target="tpu_custom_call" | custom-call | flops 4529848320 | bytes 25952256 | tf_op jit(solution)/shard_map/pallas_call | solution.py:619
  110.7 4.5 %shard_map.112 = (bf16[4,768,768]{2,1,0:T(8,128)(2,1)}, f32[4,192,768]{2,1,0:T(8,128)}, f32[4,192,768]{2,1,0:T(8,128)}, f32[4,192,768]{2,1,0:T(8,128)}) custom-call(bf16[4,768,768]{2,1,0:T(8,128)(2,1)S(1)} %get-tuple-element.8.refs_0_, f32[4,192,768]{2,1,0:T(8,128)S(1)} %get-tuple-element.9.refs_1_, f32[4,192,768]{2,1,0:T(8,128)S(1)} %get-tuple-element.10.refs_2_, ...), custom_call_target="tpu_custom_call" | custom-call | tf_op jit(solution)/shard_map/pallas_call | solution.py:632

commit v5 on v4

--- a/solution.py
+++ b/solution.py
@@ -9,7 +9,7 @@
 
 MESH = pl.DeviceIdType.MESH
 PAIR = 2
-CHUNK = 256
+CHUNK = 128
 
 
 def dot(a, b):
@@ -178,13 +178,6 @@
         for k in range(outer):
             near_copy(src, ref, s, k, sems).wait_send()
 
-    late = capacity - 1
-
-    def roots_start(s):
-        gather_start(root_right.at[s], roots, s, root_sems)
-
-    roots_start(0)
-
     order = list(range(1, outer)) + [0]
     core_copies = {}
     for k in order:
@@ -238,8 +231,7 @@
 
         lax.fori_loop(0, capacity, step, 0)
 
-    for s in range(1, late):
-        roots_start(s)
+    slots(lambda s: gather_start(root_right.at[s], roots, s, root_sems))
 
     def send_up(src, d, q):
         return remote(
@@ -429,42 +421,28 @@
         gather_start(fresh.at[s], out_weights, s, weight_sems)
         own_output(s).start()
 
-    def early(body):
-        def step(s, carry):
-            body(s)
-            return carry
-
-        lax.fori_loop(0, late, step, 0)
-
     slots(moments)
-    early(lambda s: gather_forward(roots, s, root_sems))
+    slots(lambda s: gather_forward(roots, s, root_sems))
     for q in range(chunks - 1):
         slots(lambda s: gather_forward(full, q * capacity + s, grad_sems))
-        early(functools.partial(accumulate, q))
+        slots(functools.partial(accumulate, q))
 
     def last(s, carry):
-        gather_forward(full, (chunks - 1) * capacity + s, grad_sems)
-
-        @pl.when(s >= 1)
+        @pl.when(s < capacity)
+        def _():
+            gather_forward(full, (chunks - 1) * capacity + s, grad_sems)
+
+        @pl.when((s >= 1) & (s <= capacity))
         def _():
             precondition(s - 1)
 
-        @pl.when(s == 1)
-        def _():
-            roots_start(late)
-
         @pl.when(s >= 2)
         def _():
             update(s - 2)
 
         return carry
 
-    lax.fori_loop(0, capacity, last, 0)
-    gather_forward(roots, late, root_sems)
-    for q in range(chunks - 1):
-        accumulate(q, late)
-    precondition(late)
-    update(late - 1)
+    lax.fori_loop(0, capacity + 2, last, 0)
 
     width = weights.shape[2]
     cols = width // replicas
@@ -491,10 +469,7 @@
         store(right_v, out_right, 2, s).start()
 
     slots(statistics)
-    gather_forward(out_weights, 0, weight_sems)
-    update(late)
-    for s in range(1, capacity):
-        gather_forward(out_weights, s, weight_sems)
+    slots(lambda s: gather_forward(out_weights, s, weight_sems))
 
     for copy in core_copies.values():
         copy.wait_send()

time: 115 us -> 119 us (1.035)
  Pallas kernels: 115 us -> 118 us
    pallas_call x1, Pallas kernels: 110 us -> 113 us  [on_device(): pl.pallas_call(functools.partial(kernel, replicas, owners), out_shape=tup...]
where the time goes in v5:
time: 119 us
  Pallas kernels  118 us (99%)
    pallas_call x1, Pallas kernels, on_device(): pl.pallas_call(functools.partial(kernel, replicas, owners), out_shape=tup...  113 us
    pallas_call x1, Pallas kernels, on_device(): pl.pallas_call(write_out, out_shape=tuple((pltpu.HBM(shape, dtype) for sh...  4.46 us

profile of v5, /device:TPU:0, one launch (start us, length us, event | category | flops | bytes accessed | tf_op | source)
XLA Modules:
  0.0 118.6 jit_solution(13584693288255558977)
XLA Ops:
  0.6 113.5 %shard_map.111 = (bf16[4,768,768]{2,1,0:T(8,128)(2,1)S(1)}, f32[4,192,768]{2,1,0:T(8,128)S(1)}, f32[4,192,768]{2,1,0:T(8,128)S(1)}, f32[4,192,768]{2,1,0:T(8,128)S(1)}) custom-call(s32[16]{0:T(128)} %owner_ref.1, bf16[1,2,768,768]{3,2,1,0:T(8,128)(2,1)} %grads.1, f32[4,192,768]{2,1,0:T(8,128)} %weights.1, f32[4,192,768]{2,1,0:T(8,128)} %stat_left.1, ...), custom_call_target="tpu_custom_call" | custom-call | flops 4529848320 | bytes 25952256 | tf_op jit(solution)/shard_map/pallas_call | solution.py:594
  114.1 4.5 %shard_map.112 = (bf16[4,768,768]{2,1,0:T(8,128)(2,1)}, f32[4,192,768]{2,1,0:T(8,128)}, f32[4,192,768]{2,1,0:T(8,128)}, f32[4,192,768]{2,1,0:T(8,128)}) custom-call(bf16[4,768,768]{2,1,0:T(8,128)(2,1)S(1)} %get-tuple-element.8.refs_0_, f32[4,192,768]{2,1,0:T(8,128)S(1)} %get-tuple-element.9.refs_1_, f32[4,192,768]{2,1,0:T(8,128)S(1)} %get-tuple-element.10.refs_2_, ...), custom_call_target="tpu_custom_call" | custom-call | tf_op jit(solution)/shard_map/pallas_call | solution.py:607
